TPU v7x, 32 devices: a whole 2x2x4 slice. The times are simulated.
32 devices in a mesh: groups: 2 (over y), pipe: 4 (over z), hour: 2 (over x), seg: 2 (over core).
Axes of the slice: x: 2, y: 2, z: 4, core: 2. Of those that a mesh axis runs over, the one named last changes fastest.
Arguments:
- segment_flow: float32 [16, 64, 1024], P(('groups', 'hour'), 'seg', 'pipe'), parts along dimension 0, may hold values from -4 to 4
- linepack: float32 [16, 64, 1024], P(('groups', 'hour'), 'seg', 'pipe'), parts along dimension 0, may hold values from 0.2 to 2.4
- mass_dual: float32 [16, 64, 1024], P(('groups', 'hour'), 'seg', 'pipe'), parts along dimension 0, may hold values from -3 to 3
- momentum_dual: float32 [16, 64, 1024], P(('groups', 'hour'), 'seg', 'pipe'), parts along dimension 0, may hold values from -3 to 3
- contract_dual: float32 [16, 2, 32, 128], P(('groups', 'hour'), 'seg', 'pipe'), parts along dimension 0, may hold values from -3 to 3
- flow_cost: float32 [16, 64, 1024], P(('groups', 'hour'), 'seg', 'pipe'), parts along dimension 0, may hold values from -24 to 24
- injection: float32 [16, 64, 1024], P(('groups', 'hour'), 'seg', 'pipe'), parts along dimension 0, may hold values from -3 to 3
- contract_target: float32 [16, 2, 32, 128], P(('groups', 'hour'), 'seg', 'pipe'), parts along dimension 0, may hold values from 0.4 to 2
- friction_table: float32 [16], replicated, may hold values from 0.3 to 3
- friction_class: int32 [64, 2048], P('seg', ('groups', 'pipe')), parts along dimension 1, may hold values from 0 to 15
- matching: int32 [2048], P('groups'), parts along dimension 0, may hold values from 0 to 1023, as said below
- contract_map: int32 [16, 1024], P(('groups', 'hour')), parts along dimension 0, may hold values from 0 to 127
Outputs:
- flow_final: float32 [16, 64, 1024], P(('groups', 'hour'), 'seg', 'pipe'), parts along dimension 0
- linepack_final: float32 [16, 64, 1024], P(('groups', 'hour'), 'seg', 'pipe'), parts along dimension 0
- mass_dual_final: float32 [16, 64, 1024], P(('groups', 'hour'), 'seg', 'pipe'), parts along dimension 0
- momentum_dual_final: float32 [16, 64, 1024], P(('groups', 'hour'), 'seg', 'pipe'), parts along dimension 0
- contract_dual_final: float32 [16, 2, 32, 128], P(('groups', 'hour'), 'seg', 'pipe'), parts along dimension 0
- primal_weight: float32 [2], P('groups'), parts along dimension 0
There are 2 independent parts, one for each index of `groups`. A program takes and returns all parts, laid end to end along the dimension named above; an argument that names none is the same for every part. Nothing has to cross between parts.
Inputs may be any that keep to these rules, and one draw needn't show every extreme that they name: `matching`: every pipe's inlet is fed by the outlet of exactly one pipe: each number of 0 to 1023 appears once; for any two blocks of 256 consecutive pipes, exactly 64 pipes of the first are fed from outlets of the second.
All inputs are finite; a program needn't handle non-finite values.
Results may differ from a plain program's by a relative error of at most 0.0001.
Values sent between devices are 32-bit elements; how exact they have to be, the bound alone decides.
A program may use at most 64 MiB of HBM per device.

v0:
```python
import math
import jax
import jax.numpy as jnp
from jax import lax
from jax.sharding import PartitionSpec as P

ITERS = 2
FLOW_CAP = 1.5
PACK_CAP = 2.5
STEP_SCALE = 0.25
NORM_EPS = 1e-06


def padded(cells, sides, width):
    for axis, dim in sides:
        count = lax.axis_size(axis)
        ends = count - 1
        head = lax.slice_in_dim(cells, 0, width, axis=dim)
        tail = lax.slice_in_dim(cells, cells.shape[dim] - width, cells.shape[dim], axis=dim)
        cells = jnp.concatenate(
            [
                lax.ppermute(tail, axis, [(i, (i + 1) % count) for i in range(ends)]),
                cells,
                lax.ppermute(head, axis, [((i + 1) % count, i) for i in range(ends)]),
            ],
            axis=dim,
        )
    return cells


def widened_pair(stacked):
    return padded(stacked, (("hour", 1), ("seg", 2)), 1)


def other_half(edge_row, half_index, partner_local):
    gathered = lax.all_gather(edge_row[:, None, :], ("pipe", "seg"), axis=1, tiled=True)
    hour_rows, row_count, row_width = gathered.shape
    seg_count = lax.axis_size("seg")
    picked = gathered.reshape(hour_rows, row_count // seg_count, seg_count, row_width)[
        :, :, half_index, :
    ]
    far_rows = picked.reshape(hour_rows, row_count // seg_count * row_width)
    return jnp.take(far_rows, partner_local, axis=1)


def contract_local(values, contract_rows, class_count):
    hour_rows, seg_rows, pipe_rows = values.shape
    block = math.gcd(pipe_rows, 2048)
    classes = jnp.arange(class_count, dtype=jnp.int32)

    def add_block(block_index, total):
        partial_value = lax.dynamic_slice_in_dim(values, block_index * block, block, 2)
        row_map = lax.dynamic_slice_in_dim(contract_rows, block_index * block, block, 1)
        onehot = (row_map[:, :, None] == classes[None, None, :]).astype(jnp.float32)
        return total + jnp.einsum(
            "hsp,hpc->hsc",
            partial_value,
            onehot,
            precision=lax.Precision.HIGHEST,
            preferred_element_type=jnp.float32,
        )

    return lax.fori_loop(
        0, pipe_rows // block, add_block, jnp.zeros((hour_rows, seg_rows, class_count), jnp.float32)
    )


def spread_local(duals, contract_rows):
    hour_rows, seg_rows, class_count = duals.shape
    pipe_rows = contract_rows.shape[1]
    block = math.gcd(pipe_rows, 2048)
    classes = jnp.arange(class_count, dtype=jnp.int32)

    def fill_block(block_index, result_now):
        row_map = lax.dynamic_slice_in_dim(contract_rows, block_index * block, block, 1)
        onehot = (row_map[:, :, None] == classes[None, None, :]).astype(jnp.float32)
        partial_value = jnp.einsum(
            "hsc,hpc->hsp",
            duals,
            onehot,
            precision=lax.Precision.HIGHEST,
            preferred_element_type=jnp.float32,
        )
        return lax.dynamic_update_slice_in_dim(result_now, partial_value, block_index * block, 2)

    return lax.fori_loop(
        0, pipe_rows // block, fill_block, jnp.zeros((hour_rows, seg_rows, pipe_rows), jnp.float32)
    )


def on_device(
    segment_flow,
    linepack,
    mass_dual,
    momentum_dual,
    contract_dual,
    flow_cost,
    injection,
    contract_target,
    friction_table,
    friction_class,
    matching,
    contract_map,
):
    hour_rows, seg_rows, pipe_rows = segment_flow.shape
    class_count = contract_dual.shape[3]
    pipe_count = lax.axis_size("pipe")
    total_pipes = pipe_rows * pipe_count
    share_scale = class_count / total_pipes
    pipe_start = lax.axis_index("pipe") * pipe_rows
    seg_index = lax.axis_index("seg")
    at_start = seg_index == 0
    at_end = seg_index == lax.axis_size("seg") - 1
    levels = jnp.arange(friction_table.shape[0], dtype=jnp.int32)
    friction = jnp.sum(
        jnp.where(
            friction_class[None] == levels[:, None, None], friction_table[:, None, None], 0.0
        ),
        axis=0,
    )[None]
    inverse = (
        jnp.zeros_like(matching).at[matching].set(jnp.arange(matching.shape[0], dtype=jnp.int32))
    )
    source_local = lax.dynamic_slice_in_dim(matching, pipe_start, pipe_rows)
    target_local = lax.dynamic_slice_in_dim(inverse, pipe_start, pipe_rows)
    contract_now = contract_dual.reshape(hour_rows, contract_dual.shape[2], class_count)
    target_now = contract_target.reshape(hour_rows, contract_target.shape[2], class_count)
    weight = jnp.float32(1.0)
    for iteration in range(ITERS):
        primal_step = STEP_SCALE / weight
        dual_step = STEP_SCALE * weight
        widened = widened_pair(jnp.stack([mass_dual, momentum_dual]))
        last_base = widened[0, 1:-1, -1, :]
        later_hour = widened[0, 2:, 1:-1, :]
        before_seg = widened[1, 1:-1, :-2, :]
        returned = other_half(mass_dual[:, 0, :], 0, target_local)
        last_row = last_base + jnp.where(at_end, returned, 0.0)
        next_seg = jnp.concatenate([mass_dual[:, 1:, :], last_row[:, None, :]], axis=1)
        grad_flow = mass_dual - next_seg + friction * momentum_dual
        hour_spread = spread_local(contract_now, contract_map)
        spread = lax.all_to_all(hour_spread, "pipe", split_axis=2, concat_axis=1, tiled=True)
        grad_pack = mass_dual - later_hour - momentum_dual + before_seg + share_scale * spread
        grad_flow, grad_pack = (grad_flow, grad_pack)
        flow_next = jnp.clip(
            segment_flow - primal_step * (flow_cost - grad_flow), -FLOW_CAP, FLOW_CAP
        )
        pack_next = jnp.clip(linepack + primal_step * grad_pack, 0.0, PACK_CAP)
        flow_bar = 2.0 * flow_next - segment_flow
        pack_bar = 2.0 * pack_next - linepack
        forward_widened = widened_pair(jnp.stack([flow_bar, pack_bar]))
        first_base = forward_widened[0, 1:-1, 0, :]
        earlier = forward_widened[1, :-2, 1:-1, :]
        after_seg = forward_widened[1, 1:-1, 2:, :]
        inflow = other_half(flow_bar[:, -1, :], 1, source_local)
        first_row = first_base + jnp.where(at_start, inflow, 0.0)
        upstream = jnp.concatenate([first_row[:, None, :], flow_bar[:, :-1, :]], axis=1)
        mass_rows = pack_bar - earlier + flow_bar - upstream
        momentum = friction * flow_bar - (pack_bar - after_seg)
        hour_major = lax.all_to_all(pack_bar, "pipe", split_axis=1, concat_axis=2, tiled=True)
        totals = contract_local(hour_major, contract_map, class_count)
        mass_rows, momentum, totals = (mass_rows, momentum, share_scale * totals)
        mass_next = mass_dual + dual_step * (injection - mass_rows)
        momentum_next = momentum_dual - dual_step * momentum
        contract_next = contract_now + dual_step * (target_now - totals)
        primal_sq = jnp.sum((flow_next - segment_flow) ** 2) + jnp.sum((pack_next - linepack) ** 2)
        dual_sq = (
            jnp.sum((mass_next - mass_dual) ** 2)
            + jnp.sum((momentum_next - momentum_dual) ** 2)
            + jnp.sum((contract_next - contract_now) ** 2)
        )
        primal_total, dual_total = lax.psum((primal_sq, dual_sq), ("pipe", "hour", "seg"))
        weight = jnp.sqrt(weight * jnp.sqrt((dual_total + NORM_EPS) / (primal_total + NORM_EPS)))
        segment_flow, linepack = (flow_next, pack_next)
        mass_dual, momentum_dual, contract_now = (mass_next, momentum_next, contract_next)
    return (
        segment_flow,
        linepack,
        mass_dual,
        momentum_dual,
        contract_now.reshape(contract_dual.shape),
        weight.reshape(1),
    )


def solution(mesh):
    return jax.shard_map(
        on_device,
        mesh=mesh,
        in_specs=(
            P(("groups", "hour"), "seg", "pipe"),
            P(("groups", "hour"), "seg", "pipe"),
            P(("groups", "hour"), "seg", "pipe"),
            P(("groups", "hour"), "seg", "pipe"),
            P(("groups", "hour"), "seg", "pipe", None),
            P(("groups", "hour"), "seg", "pipe"),
            P(("groups", "hour"), "seg", "pipe"),
            P(("groups", "hour"), "seg", "pipe", None),
            P(),
            P("seg", ("groups", "pipe")),
            P("groups"),
            P(("groups", "hour"), None),
        ),
        out_specs=(
            P(("groups", "hour"), "seg", "pipe"),
            P(("groups", "hour"), "seg", "pipe"),
            P(("groups", "hour"), "seg", "pipe"),
            P(("groups", "hour"), "seg", "pipe"),
            P(("groups", "hour"), "seg", "pipe", None),
            P("groups"),
        ),
        check_vma=False,
    )
```

profile of v0, /device:TPU:0, one launch (start us, length us, event | category | flops | bytes accessed | tf_op | source)
XLA Modules:
  0.0 255.9 jit_solution(9958504613072737630)
XLA Ops:
  0.6 2.2 fusion.4
  2.9 0.8 copy.144
  3.7 3.1 %reshape.116 = f32[4,1,8192]{2,1,0:T(1,128)} reshape(f32[1024,4,8]{2,1,0:T(4,128)S(1)} %bitcast.195) | data formatting | bytes 262144
  6.8 6.3 %all-to-all-start = ((f32[4,1,8192]{2,1,0:T(1,128)}), f32[4,1,8192]{2,1,0:T(1,128)S(1)}, u32[]{:S(2)}, u32[]{:S(2)}) async-start(f32[4,1,8192]{2,1,0:T(1,128)} %reshape.116), calls=%async_computation | async-start | bytes 262144 | tf_op jit(solution)/shard_map/all_to_all | solution.py:141
  13.2 1.3 collective-permute-start.1
  14.5 4.5 %collective-permute-start = (f32[2,1,32,256]{3,2,1,0:T(8,128)S(1)}, f32[2,1,32,256]{3,2,1,0:T(8,128)S(1)}, u32[]{:S(2)}, u32[]{:S(2)}) collective-permute-start(f32[2,1,32,256]{3,2,1,0:T(8,128)S(1)} %get-tuple-element.135), channel_id=1, source_target_pairs={{0,2},{1,3},{4,6},{5,7},{8,10},{9,11},{12,14},{13,15},{16,18},{17,... | collective-permute-start | bytes 196616 | tf_op jit(solution)/shard_map/ppermute | solution.py:22
  19.1 14.6 %all_gather.12 = f32[4,8,256]{2,0,1:T(4,128)S(1)} all-gather(f32[4,1,256]{2,0,1:T(4,128)S(1)} %copy.255), channel_id=1, replica_groups=mesh['groups'=2,'pipe'=4,'hour'=2,'seg'=2] {'pipe','seg'}, dimensions={1}, use_global_device_ids=true | all-gather | bytes 36864 | tf_op jit(solution)/shard_map/all_gather | solution.py:36
  33.9 4.3 %scatter_custom_fusion = s32[1024]{0:T(1024)S(1)} fusion(s32[1024]{0:T(1024)S(1)} %compare_select_fusion, s32[1024]{0:T(1024)S(1)} %iota.14, s32[]{:T(128)} %constant.26.clone.1), kind=kCustom, calls=%fused_computation.140 | custom fusion | bytes 4100 | tf_op jit(solution)/shard_map/scatter | solution.py:122
  38.3 0.7 copy.256
  39.2 0.7 gather_fusion
  40.3 2.2 collective-permute-start.3
  42.7 1.3 collective-permute-start.2
  44.6 1.5 collective-permute-done.2
  46.8 1.0 reduce
  47.8 2.5 reshape.117
  50.4 1.8 broadcast_multiply_fusion.1
  52.2 1.9 copy.145
  54.1 1.2 multiply_reduce_fusion.4
  55.4 0.8 multiply_subtract_fusion.3
  56.3 0.9 copy_dynamic-update-slice_fusion.4
  57.2 1.4 collective-permute-start.5
  58.7 4.5 %collective-permute-start.4 = (f32[2,1,32,256]{3,2,1,0:T(8,128)S(1)}, f32[2,1,32,256]{3,2,1,0:T(8,128)S(1)}, u32[]{:S(2)}, u32[]{:S(2)}) collective-permute-start(f32[2,1,32,256]{3,2,1,0:T(8,128)S(1)} %get-tuple-element.131), channel_id=1, source_target_pairs={{0,2},{1,3},{4,6},{5,7},{8,10},{9,11},{12,14},{13,15},{16,18},{17,... | collective-permute-start | bytes 196616 | tf_op jit(solution)/shard_map/ppermute | solution.py:22
  63.3 14.0 %all_gather.13 = f32[4,8,256]{2,0,1:T(4,128)S(1)} all-gather(f32[4,1,256]{2,0,1:T(4,128)S(1)} %slice.182), channel_id=1, replica_groups=mesh['groups'=2,'pipe'=4,'hour'=2,'seg'=2] {'pipe','seg'}, dimensions={1}, use_global_device_ids=true | all-gather | bytes 36864 | tf_op jit(solution)/shard_map/all_gather | solution.py:36
  77.5 0.7 gather_fusion.1
  78.7 2.2 collective-permute-start.6
  81.0 1.5 collective-permute-start.7
  82.7 1.4 collective-permute-done.7
  84.0 2.0 multiply_reduce_fusion.7
  86.2 1.3 collective-permute-start.9
  87.5 4.5 %collective-permute-start.8 = (f32[2,1,32,256]{3,2,1,0:T(8,128)S(1)}, f32[2,1,32,256]{3,2,1,0:T(8,128)S(1)}, u32[]{:S(2)}, u32[]{:S(2)}) collective-permute-start(f32[2,1,32,256]{3,2,1,0:T(8,128)S(1)} %get-tuple-element.127), channel_id=1, source_target_pairs={{0,2},{1,3},{4,6},{5,7},{8,10},{9,11},{12,14},{13,15},{16,18},{17,... | collective-permute-start | bytes 196616 | tf_op jit(solution)/shard_map/ppermute | solution.py:22
  92.0 4.5 %all-to-all-start.1 = ((f32[4,32,256]{2,0,1:T(4,128)}), f32[4,32,256]{2,0,1:T(4,128)S(1)}, u32[]{:S(2)}, u32[]{:S(2)}) async-start(f32[4,32,256]{2,0,1:T(4,128)} %multiply_subtract_fusion.3), calls=%async_computation.1 | async-start | bytes 262144 | tf_op jit(solution)/shard_map/all_to_all | solution.py:159
  98.5 14.6 %all_gather.14 = f32[4,8,256]{2,0,1:T(4,128)S(1)} all-gather(f32[4,1,256]{2,0,1:T(4,128)S(1)} %slice.191), channel_id=1, replica_groups=mesh['groups'=2,'pipe'=4,'hour'=2,'seg'=2] {'pipe','seg'}, dimensions={1}, use_global_device_ids=true | all-gather | bytes 36864 | tf_op jit(solution)/shard_map/all_gather | solution.py:36
  113.3 1.3 gather_fusion.2
  116.3 2.2 collective-permute-start.11
  118.5 0.9 copy.197
  119.3 1.3 collective-permute-start.10
  120.7 2.2 fusion.73
  122.9 1.8 fusion.1
  124.8 0.8 copy.174
  125.6 3.1 %reshape.118 = f32[4,1,8192]{2,1,0:T(1,128)} reshape(f32[1024,4,8]{2,1,0:T(4,128)S(1)} %bitcast.197) | data formatting | bytes 262144
  128.7 4.5 %all-to-all-start.2 = ((f32[4,1,8192]{2,1,0:T(1,128)}), f32[4,1,8192]{2,1,0:T(1,128)S(1)}, u32[]{:S(2)}, u32[]{:S(2)}) async-start(f32[4,1,8192]{2,1,0:T(1,128)} %reshape.118), calls=%async_computation.2 | async-start | bytes 262144 | tf_op jit(solution)/shard_map/all_to_all | solution.py:141
  133.2 1.1 fusion.31
  135.1 33.5 %all-reduce.1 = (f32[]{:T(128)}, f32[]{:T(128)}) all-reduce(f32[]{:T(128)S(6)} %add.153, f32[]{:T(128)S(6)} %add.155), channel_id=1, replica_groups=mesh['groups'=2,'pipe'=4,'hour'=2,'seg'=2] {'pipe','hour','seg'}, use_global_device_ids=true, to_apply=%region_5.7 | all-reduce | flops 2 | bytes 16 | tf_op jit(solution)/shard_map/psum | solution.py:171
  170.1 1.0 reduce.1
  171.0 2.5 reshape.119
  173.6 1.8 broadcast_multiply_fusion
  175.4 1.9 copy.175
  177.3 0.9 multiply_reduce_fusion
  178.2 0.7 multiply_subtract_fusion.1
  179.0 0.9 copy_dynamic-update-slice_fusion
  180.0 1.3 collective-permute-start.13
  181.3 4.5 %collective-permute-start.12 = (f32[2,1,32,256]{3,2,1,0:T(8,128)S(1)}, f32[2,1,32,256]{3,2,1,0:T(8,128)S(1)}, u32[]{:S(2)}, u32[]{:S(2)}) collective-permute-start(f32[2,1,32,256]{3,2,1,0:T(8,128)S(1)} %get-tuple-element.123), channel_id=1, source_target_pairs={{0,2},{1,3},{4,6},{5,7},{8,10},{9,11},{12,14},{13,15},{16,18},{17,... | collective-permute-start | bytes 196616 | tf_op jit(solution)/shard_map/ppermute | solution.py:22
  185.8 0.7 copy.186
  186.5 0.7 copy.187
  187.2 3.5 %all-to-all-start.3 = ((f32[4,32,256]{2,0,1:T(4,128)}), f32[4,32,256]{2,0,1:T(4,128)S(1)}, u32[]{:S(2)}, u32[]{:S(2)}) async-start(f32[4,32,256]{2,0,1:T(4,128)} %multiply_subtract_fusion.1), calls=%async_computation.3 | async-start | bytes 262144 | tf_op jit(solution)/shard_map/all_to_all | solution.py:159
  190.7 14.6 %all_gather.15 = f32[4,8,256]{2,0,1:T(4,128)S(1)} all-gather(f32[4,1,256]{2,0,1:T(4,128)S(1)} %slice.198), channel_id=1, replica_groups=mesh['groups'=2,'pipe'=4,'hour'=2,'seg'=2] {'pipe','seg'}, dimensions={1}, use_global_device_ids=true | all-gather | bytes 36864 | tf_op jit(solution)/shard_map/all_gather | solution.py:36
  205.6 0.7 gather_fusion.3
  207.9 1.3 collective-permute-start.15
  209.4 3.0 %collective-permute-start.14 = (f32[2,6,1,256]{1,3,2,0:T(8,128)S(1)}, f32[2,6,1,256]{1,3,2,0:T(8,128)S(1)}, u32[]{:S(2)}, u32[]{:S(2)}) collective-permute-start(f32[2,6,1,256]{1,3,2,0:T(8,128)S(1)} %copy.201), channel_id=1, source_target_pairs={{0,1},{2,3},{4,5},{6,7},{8,9},{10,11},{12,13},{14,15},{16,17},{18,... | collective-permute-start | bytes 36872 | tf_op jit(solution)/shard_map/ppermute | solution.py:22
  212.4 1.1 collective-permute-done.14
  213.8 1.8 multiply_reduce_fusion.2
  217.6 2.4 multiply_reduce_fusion.8
  220.7 0.7 copy.189
  221.4 32.0 %all-reduce = (f32[]{:T(128)}, f32[]{:T(128)}) all-reduce(f32[]{:T(128)S(6)} %add.167, f32[]{:T(128)S(6)} %add.169), channel_id=1, replica_groups=mesh['groups'=2,'pipe'=4,'hour'=2,'seg'=2] {'pipe','hour','seg'}, use_global_device_ids=true, to_apply=%region_12.14 | all-reduce | flops 2 | bytes 16 | tf_op jit(solution)/shard_map/psum | solution.py:171
  (119 shorter events, 6.6 us)
Async XLA Ops:
  2.8 10.3 %copy-start = (f32[4,32,256]{2,1,0:T(8,128)S(1)}, f32[4,32,256]{2,1,0:T(8,128)}, u32[]{:S(2)}) copy-start(f32[4,32,256]{2,1,0:T(8,128)} %param.16) | copy-start | bytes 393220
  2.8 10.3 %copy-start.1 = (f32[4,32,256]{2,1,0:T(8,128)S(1)}, f32[4,32,256]{2,1,0:T(8,128)}, u32[]{:S(2)}) copy-start(f32[4,32,256]{2,1,0:T(8,128)} %param.17) | copy-start | bytes 393220
  3.7 30.2 %copy-start.12 = (s32[1024]{0:T(1024)S(1)}, s32[1024]{0:T(1024)}, u32[]{:S(2)}) copy-start(s32[1024]{0:T(1024)} %param.24) | copy-start | bytes 12292
  3.7 35.3 %copy-start.11 = (s32[32,256]{1,0:T(8,128)S(1)}, s32[32,256]{1,0:T(8,128)}, u32[]{:S(2)}) copy-start(s32[32,256]{1,0:T(8,128)} %param.23) | copy-start | bytes 98308
  3.7 35.3 %copy-start.13 = (f32[16]{0:T(128)S(1)}, f32[16]{0:T(128)}, u32[]{:S(2)}) copy-start(f32[16]{0:T(128)} %param.22) | copy-start | bytes 196
  6.8 39.5 %all-to-all-start = ((f32[4,1,8192]{2,1,0:T(1,128)}), f32[4,1,8192]{2,1,0:T(1,128)S(1)}, u32[]{:S(2)}, u32[]{:S(2)}) async-start(f32[4,1,8192]{2,1,0:T(1,128)} %reshape.116), calls=%async_computation | async-start | bytes 262144 | tf_op jit(solution)/shard_map/all_to_all | solution.py:141
  13.2 26.8 %collective-permute-start.1 = (f32[2,1,32,256]{3,2,1,0:T(8,128)S(1)}, f32[2,1,32,256]{3,2,1,0:T(8,128)S(1)}, u32[]{:S(2)}, u32[]{:S(2)}) collective-permute-start(f32[2,1,32,256]{3,2,1,0:T(8,128)S(1)} %get-tuple-element.136), channel_id=1, source_target_pairs={{2,0},{3,1},{6,4},{7,5},{10,8},{11,9},{14,12},{15,13},{18,16},{19,... | collective-permute-start | bytes 196616 | tf_op jit(solution)/shard_map/ppermute | solution.py:24
  14.5 25.5 %collective-permute-start = (f32[2,1,32,256]{3,2,1,0:T(8,128)S(1)}, f32[2,1,32,256]{3,2,1,0:T(8,128)S(1)}, u32[]{:S(2)}, u32[]{:S(2)}) collective-permute-start(f32[2,1,32,256]{3,2,1,0:T(8,128)S(1)} %get-tuple-element.135), channel_id=1, source_target_pairs={{0,2},{1,3},{4,6},{5,7},{8,10},{9,11},{12,14},{13,15},{16,18},{17,... | collective-permute-start | bytes 196616 | tf_op jit(solution)/shard_map/ppermute | solution.py:22
  40.3 13.8 %collective-permute-start.3 = (f32[2,6,1,256]{3,1,2,0:T(8,128)S(1)}, f32[2,6,1,256]{3,1,2,0:T(8,128)S(1)}, u32[]{:S(2)}, u32[]{:S(2)}) collective-permute-start(f32[2,6,1,256]{3,1,2,0:T(8,128)S(1)} %slice.177), channel_id=1, source_target_pairs={{0,1},{2,3},{4,5},{6,7},{8,9},{10,11},{12,13},{14,15},{16,17},{18,... | collective-permute-start | bytes 36872 | tf_op jit(solution)/shard_map/ppermute | solution.py:22
  42.7 3.4 %collective-permute-start.2 = (f32[2,6,1,256]{1,3,2,0:T(8,128)S(1)}, f32[2,6,1,256]{1,3,2,0:T(8,128)S(1)}, u32[]{:S(2)}, u32[]{:S(2)}) collective-permute-start(f32[2,6,1,256]{1,3,2,0:T(8,128)S(1)} %copy.191), channel_id=1, source_target_pairs={{1,0},{3,2},{5,4},{7,6},{9,8},{11,10},{13,12},{15,14},{17,16},{19,... | collective-permute-start | bytes 36872 | tf_op jit(solution)/shard_map/ppermute | solution.py:24
  52.1 1.9 copy-start.2
  52.2 2.0 copy-start.3
  52.2 2.0 copy-start.4
  52.2 2.0 copy-start.8
  52.2 2.0 copy-start.9
  57.2 26.8 %copy-start.6 = (f32[4,32,256]{2,1,0:T(8,128)S(1)}, f32[4,32,256]{2,1,0:T(8,128)}, u32[]{:S(2)}) copy-start(f32[4,32,256]{2,1,0:T(8,128)} %param.20) | copy-start | bytes 393220
  57.2 21.0 %collective-permute-start.5 = (f32[2,1,32,256]{3,2,1,0:T(8,128)S(1)}, f32[2,1,32,256]{3,2,1,0:T(8,128)S(1)}, u32[]{:S(2)}, u32[]{:S(2)}) collective-permute-start(f32[2,1,32,256]{3,2,1,0:T(8,128)S(1)} %get-tuple-element.132), channel_id=1, source_target_pairs={{2,0},{3,1},{6,4},{7,5},{10,8},{11,9},{14,12},{15,13},{18,16},{19,... | collective-permute-start | bytes 196616 | tf_op jit(solution)/shard_map/ppermute | solution.py:24
  58.7 19.6 %collective-permute-start.4 = (f32[2,1,32,256]{3,2,1,0:T(8,128)S(1)}, f32[2,1,32,256]{3,2,1,0:T(8,128)S(1)}, u32[]{:S(2)}, u32[]{:S(2)}) collective-permute-start(f32[2,1,32,256]{3,2,1,0:T(8,128)S(1)} %get-tuple-element.131), channel_id=1, source_target_pairs={{0,2},{1,3},{4,6},{5,7},{8,10},{9,11},{12,14},{13,15},{16,18},{17,... | collective-permute-start | bytes 196616 | tf_op jit(solution)/shard_map/ppermute | solution.py:22
  78.7 3.7 %collective-permute-start.6 = (f32[2,6,1,256]{1,3,2,0:T(8,128)S(1)}, f32[2,6,1,256]{1,3,2,0:T(8,128)S(1)}, u32[]{:S(2)}, u32[]{:S(2)}) collective-permute-start(f32[2,6,1,256]{1,3,2,0:T(8,128)S(1)} %copy.195), channel_id=1, source_target_pairs={{0,1},{2,3},{4,5},{6,7},{8,9},{10,11},{12,13},{14,15},{16,17},{18,... | collective-permute-start | bytes 36872 | tf_op jit(solution)/shard_map/ppermute | solution.py:22
  81.0 3.1 %collective-permute-start.7 = (f32[2,6,1,256]{3,1,2,0:T(8,128)S(1)}, f32[2,6,1,256]{3,1,2,0:T(8,128)S(1)}, u32[]{:S(2)}, u32[]{:S(2)}) collective-permute-start(f32[2,6,1,256]{3,1,2,0:T(8,128)S(1)} %slice.185), channel_id=1, source_target_pairs={{1,0},{3,2},{5,4},{7,6},{9,8},{11,10},{13,12},{15,14},{17,16},{19,... | collective-permute-start | bytes 36872 | tf_op jit(solution)/shard_map/ppermute | solution.py:24
  86.1 34.6 %copy-start.14 = (f32[4,1,8,128]{3,2,1,0:T(8,128)S(1)}, f32[4,1,8,128]{3,2,1,0:T(8,128)}, u32[]{:S(2)}) copy-start(f32[4,1,8,128]{3,2,1,0:T(8,128)} %param.18) | copy-start | bytes 49156
  86.1 34.6 %copy-start.15 = (s32[4,1024]{1,0:T(4,128)S(1)}, s32[4,1024]{1,0:T(4,128)}, u32[]{:S(2)}) copy-start(s32[4,1024]{1,0:T(4,128)} %param.25) | copy-start | bytes 49156
  86.1 34.6 %copy-start.16 = (f32[4,1,8,128]{3,2,1,0:T(8,128)S(1)}, f32[4,1,8,128]{3,2,1,0:T(8,128)}, u32[]{:S(2)}) copy-start(f32[4,1,8,128]{3,2,1,0:T(8,128)} %param.21) | copy-start | bytes 49156
  86.2 29.8 %collective-permute-start.9 = (f32[2,1,32,256]{3,2,1,0:T(8,128)S(1)}, f32[2,1,32,256]{3,2,1,0:T(8,128)S(1)}, u32[]{:S(2)}, u32[]{:S(2)}) collective-permute-start(f32[2,1,32,256]{3,2,1,0:T(8,128)S(1)} %get-tuple-element.128), channel_id=1, source_target_pairs={{2,0},{3,1},{6,4},{7,5},{10,8},{11,9},{14,12},{15,13},{18,16},{19,... | collective-permute-start | bytes 196616 | tf_op jit(solution)/shard_map/ppermute | solution.py:24
  87.5 28.5 %collective-permute-start.8 = (f32[2,1,32,256]{3,2,1,0:T(8,128)S(1)}, f32[2,1,32,256]{3,2,1,0:T(8,128)S(1)}, u32[]{:S(2)}, u32[]{:S(2)}) collective-permute-start(f32[2,1,32,256]{3,2,1,0:T(8,128)S(1)} %get-tuple-element.127), channel_id=1, source_target_pairs={{0,2},{1,3},{4,6},{5,7},{8,10},{9,11},{12,14},{13,15},{16,18},{17,... | collective-permute-start | bytes 196616 | tf_op jit(solution)/shard_map/ppermute | solution.py:22
  92.0 28.6 %all-to-all-start.1 = ((f32[4,32,256]{2,0,1:T(4,128)}), f32[4,32,256]{2,0,1:T(4,128)S(1)}, u32[]{:S(2)}, u32[]{:S(2)}) async-start(f32[4,32,256]{2,0,1:T(4,128)} %multiply_subtract_fusion.3), calls=%async_computation.1 | async-start | bytes 262144 | tf_op jit(solution)/shard_map/all_to_all | solution.py:159
  116.3 61.0 %collective-permute-start.11 = (f32[2,6,1,256]{3,1,2,0:T(8,128)S(1)}, f32[2,6,1,256]{3,1,2,0:T(8,128)S(1)}, u32[]{:S(2)}, u32[]{:S(2)}) collective-permute-start(f32[2,6,1,256]{3,1,2,0:T(8,128)S(1)} %slice.193), channel_id=1, source_target_pairs={{0,1},{2,3},{4,5},{6,7},{8,9},{10,11},{12,13},{14,15},{16,17},{18,... | collective-permute-start | bytes 36872 | tf_op jit(solution)/shard_map/ppermute | solution.py:22
  119.3 13.9 %collective-permute-start.10 = (f32[2,6,1,256]{1,3,2,0:T(8,128)}, f32[2,6,1,256]{1,3,2,0:T(8,128)}, u32[]{:S(2)}, u32[]{:S(2)}) collective-permute-start(f32[2,6,1,256]{1,3,2,0:T(8,128)} %copy.197), channel_id=1, source_target_pairs={{1,0},{3,2},{5,4},{7,6},{9,8},{11,10},{13,12},{15,14},{17,16},{19,... | collective-permute-start | bytes 36872 | tf_op jit(solution)/shard_map/ppermute | solution.py:24
  128.7 41.3 %all-to-all-start.2 = ((f32[4,1,8192]{2,1,0:T(1,128)}), f32[4,1,8192]{2,1,0:T(1,128)S(1)}, u32[]{:S(2)}, u32[]{:S(2)}) async-start(f32[4,1,8192]{2,1,0:T(1,128)} %reshape.118), calls=%async_computation.2 | async-start | bytes 262144 | tf_op jit(solution)/shard_map/all_to_all | solution.py:141
  175.4 1.9 copy-start.5
  175.4 1.9 copy-start.10
  180.0 27.6 %collective-permute-start.13 = (f32[2,1,32,256]{3,2,1,0:T(8,128)S(1)}, f32[2,1,32,256]{3,2,1,0:T(8,128)S(1)}, u32[]{:S(2)}, u32[]{:S(2)}) collective-permute-start(f32[2,1,32,256]{3,2,1,0:T(8,128)S(1)} %get-tuple-element.124), channel_id=1, source_target_pairs={{2,0},{3,1},{6,4},{7,5},{10,8},{11,9},{14,12},{15,13},{18,16},{19,... | collective-permute-start | bytes 196616 | tf_op jit(solution)/shard_map/ppermute | solution.py:24
  181.3 26.3 %collective-permute-start.12 = (f32[2,1,32,256]{3,2,1,0:T(8,128)S(1)}, f32[2,1,32,256]{3,2,1,0:T(8,128)S(1)}, u32[]{:S(2)}, u32[]{:S(2)}) collective-permute-start(f32[2,1,32,256]{3,2,1,0:T(8,128)S(1)} %get-tuple-element.123), channel_id=1, source_target_pairs={{0,2},{1,3},{4,6},{5,7},{8,10},{9,11},{12,14},{13,15},{16,18},{17,... | collective-permute-start | bytes 196616 | tf_op jit(solution)/shard_map/ppermute | solution.py:22
  187.2 26.6 %copy-start.7 = (f32[4,32,256]{2,1,0:T(8,128)S(1)}, f32[4,32,256]{2,1,0:T(8,128)}, u32[]{:S(2)}) copy-start(f32[4,32,256]{2,1,0:T(8,128)} %param.20) | copy-start | bytes 393220
  187.2 30.4 %all-to-all-start.3 = ((f32[4,32,256]{2,0,1:T(4,128)}), f32[4,32,256]{2,0,1:T(4,128)S(1)}, u32[]{:S(2)}, u32[]{:S(2)}) async-start(f32[4,32,256]{2,0,1:T(4,128)} %multiply_subtract_fusion.1), calls=%async_computation.3 | async-start | bytes 262144 | tf_op jit(solution)/shard_map/all_to_all | solution.py:159
  207.9 5.8 %collective-permute-start.15 = (f32[2,6,1,256]{3,1,2,0:T(8,128)S(1)}, f32[2,6,1,256]{3,1,2,0:T(8,128)S(1)}, u32[]{:S(2)}, u32[]{:S(2)}) collective-permute-start(f32[2,6,1,256]{3,1,2,0:T(8,128)S(1)} %slice.201), channel_id=1, source_target_pairs={{1,0},{3,2},{5,4},{7,6},{9,8},{11,10},{13,12},{15,14},{17,16},{19,... | collective-permute-start | bytes 36872 | tf_op jit(solution)/shard_map/ppermute | solution.py:24
  209.4 4.2 %collective-permute-start.14 = (f32[2,6,1,256]{1,3,2,0:T(8,128)S(1)}, f32[2,6,1,256]{1,3,2,0:T(8,128)S(1)}, u32[]{:S(2)}, u32[]{:S(2)}) collective-permute-start(f32[2,6,1,256]{1,3,2,0:T(8,128)S(1)} %copy.201), channel_id=1, source_target_pairs={{0,1},{2,3},{4,5},{6,7},{8,9},{10,11},{12,13},{14,15},{16,17},{18,... | collective-permute-start | bytes 36872 | tf_op jit(solution)/shard_map/ppermute | solution.py:22
where the time goes:
time: 257 us; the launch traced here: 256 us
  blocking collectives  123 us (48%)
  starting transfers between devices  57.3 us (22%)
  local copies, waits for them, and re-layouts  34.9 us (14%)
  other arithmetic  15.8 us (6%)
  between operations  12.1 us (5%)
  matrix products  8.66 us (3%)
  waiting for transfers between devices  3.97 us (2%)
    psum x2, blocking collectives, on_device(): lax.psum((primal_sq, dual_sq), ('pipe', 'hour', 'seg'))  65.5 us
    all_gather x4, blocking collectives, other_half(): lax.all_gather(edge_row[:, None, :], ('pipe', 'seg'), axis=1, tiled=True)  57.8 us
    ppermute x8, starting transfers between devices, padded(): lax.ppermute(tail, axis, [(i, (i + 1) % count) for i in range(ends)])  27.9 us
    unnamed x55, local copies, waits for them, and re-layouts  17 us
    all_to_all x2, starting transfers between devices, on_device(): lax.all_to_all(hour_spread, 'pipe', split_axis=2, concat_axis=1, tiled=True)  10.8 us
    ppermute x8, starting transfers between devices, padded(): lax.ppermute(head, axis, [((i + 1) % count, i) for i in range(ends)])  10.6 us
    all_to_all x2, starting transfers between devices, on_device(): lax.all_to_all(pack_bar, 'pipe', split_axis=1, concat_axis=2, tiled=True)  7.96 us
  transfers between devices with their start and end apart: 20, of which 3 were waited for; matrix products, arithmetic and copies ran while one was open for 16% of the time, Pallas kernels for 0%

commit v1 on v0

--- a/solution.py
+++ b/solution.py
@@ -3,6 +3,7 @@
 import jax.numpy as jnp
 from jax import lax
 from jax.sharding import PartitionSpec as P
+from jax.lax import psum
 
 ITERS = 2
 FLOW_CAP = 1.5
@@ -168,7 +169,9 @@
             + jnp.sum((momentum_next - momentum_dual) ** 2)
             + jnp.sum((contract_next - contract_now) ** 2)
         )
-        primal_total, dual_total = lax.psum((primal_sq, dual_sq), ("pipe", "hour", "seg"))
+        primal_total, dual_total = psum(
+            psum((primal_sq, dual_sq), axis_name=("hour", "seg")), axis_name="pipe"
+        )
         weight = jnp.sqrt(weight * jnp.sqrt((dual_total + NORM_EPS) / (primal_total + NORM_EPS)))
         segment_flow, linepack = (flow_next, pack_next)
         mass_dual, momentum_dual, contract_now = (mass_next, momentum_next, contract_next)

time: 257 us -> 231 us (0.90)
  blocking collectives: 123 us -> 96.6 us
    psum x2 -> x4, blocking collectives: 65.5 us -> 38.8 us  [the longest x2 24.6 us: on_device(): psum(psum((primal_sq, dual_sq), axis_name=('hour', 'seg')), axis_name='pi...]
  transfers between devices with their start and end apart: 20 -> 20, of which waited for: 3 -> 3; matrix products, arithmetic and copies ran while one was open for 16% -> 18% of each run, Pallas kernels for 0% -> 0%
where the time goes in v1:
time: 231 us; the launch traced here: 229 us
  blocking collectives  96.6 us (42%)
  starting transfers between devices  57.3 us (25%)
  local copies, waits for them, and re-layouts  35.1 us (15%)
  other arithmetic  15.6 us (7%)
  between operations  11.9 us (5%)
  matrix products  8.93 us (4%)
  waiting for transfers between devices  3.97 us (2%)
    all_gather x4, blocking collectives, other_half(): lax.all_gather(edge_row[:, None, :], ('pipe', 'seg'), axis=1, tiled=True)  57.8 us
    ppermute x8, starting transfers between devices, padded(): lax.ppermute(tail, axis, [(i, (i + 1) % count) for i in range(ends)])  27.9 us
    psum x2, blocking collectives, on_device(): psum(psum((primal_sq, dual_sq), axis_name=('hour', 'seg')), axis_name='pi...  24.6 us
    unnamed x55, local copies, waits for them, and re-layouts  17 us
    psum x2, blocking collectives, on_device(): psum((primal_sq, dual_sq), axis_name=('hour', 'seg'))  14.2 us
    all_to_all x2, starting transfers between devices, on_device(): lax.all_to_all(hour_spread, 'pipe', split_axis=2, concat_axis=1, tiled=True)  10.8 us
    ppermute x8, starting transfers between devices, padded(): lax.ppermute(head, axis, [((i + 1) % count, i) for i in range(ends)])  10.6 us
    all_to_all x2, starting transfers between devices, on_device(): lax.all_to_all(pack_bar, 'pipe', split_axis=1, concat_axis=2, tiled=True)  7.96 us
  transfers between devices with their start and end apart: 20, of which 3 were waited for; matrix products, arithmetic and copies ran while one was open for 18% of the time, Pallas kernels for 0%

profile of v1, /device:TPU:0, one launch (start us, length us, event | category | flops | bytes accessed | tf_op | source)
XLA Modules:
  0.0 229.4 jit_solution(2815113595825467222)
XLA Ops:
  0.6 2.2 fusion.4
  2.9 0.8 copy.144
  3.7 3.1 %reshape.116 = f32[4,1,8192]{2,1,0:T(1,128)} reshape(f32[1024,4,8]{2,1,0:T(4,128)S(1)} %bitcast.195) | data formatting | bytes 262144
  6.8 6.3 %all-to-all-start = ((f32[4,1,8192]{2,1,0:T(1,128)}), f32[4,1,8192]{2,1,0:T(1,128)S(1)}, u32[]{:S(2)}, u32[]{:S(2)}) async-start(f32[4,1,8192]{2,1,0:T(1,128)} %reshape.116), calls=%async_computation | async-start | bytes 262144 | tf_op jit(solution)/shard_map/all_to_all | solution.py:142
  13.2 1.3 collective-permute-start.1
  14.5 4.5 %collective-permute-start = (f32[2,1,32,256]{3,2,1,0:T(8,128)S(1)}, f32[2,1,32,256]{3,2,1,0:T(8,128)S(1)}, u32[]{:S(2)}, u32[]{:S(2)}) collective-permute-start(f32[2,1,32,256]{3,2,1,0:T(8,128)S(1)} %get-tuple-element.139), channel_id=1, source_target_pairs={{0,2},{1,3},{4,6},{5,7},{8,10},{9,11},{12,14},{13,15},{16,18},{17,... | collective-permute-start | bytes 196616 | tf_op jit(solution)/shard_map/ppermute | solution.py:23
  19.1 14.6 %all_gather.12 = f32[4,8,256]{2,0,1:T(4,128)S(1)} all-gather(f32[4,1,256]{2,0,1:T(4,128)S(1)} %copy.255), channel_id=1, replica_groups=mesh['groups'=2,'pipe'=4,'hour'=2,'seg'=2] {'pipe','seg'}, dimensions={1}, use_global_device_ids=true | all-gather | bytes 36864 | tf_op jit(solution)/shard_map/all_gather | solution.py:37
  33.9 4.3 %scatter_custom_fusion = s32[1024]{0:T(1024)S(1)} fusion(s32[1024]{0:T(1024)S(1)} %compare_select_fusion, s32[1024]{0:T(1024)S(1)} %iota.14, s32[]{:T(128)} %constant.26.clone.1), kind=kCustom, calls=%fused_computation.140 | custom fusion | bytes 4100 | tf_op jit(solution)/shard_map/scatter | solution.py:123
  38.3 0.7 copy.256
  39.2 0.7 gather_fusion
  40.3 2.2 collective-permute-start.3
  42.7 1.3 collective-permute-start.2
  44.6 1.5 collective-permute-done.2
  46.8 1.0 reduce
  47.8 2.5 %reshape.117 = f32[1024,4,8]{2,1,0:T(4,128)S(1)} reshape(f32[4,8192]{1,0:T(4,128)S(1)} %reduce) | data formatting | bytes 262144
  50.4 1.8 broadcast_multiply_fusion.1
  52.2 1.9 copy.145
  54.1 1.2 multiply_reduce_fusion.4
  55.3 0.8 multiply_subtract_fusion.3
  56.2 0.9 copy_dynamic-update-slice_fusion.4
  57.2 1.4 collective-permute-start.5
  58.6 4.5 %collective-permute-start.4 = (f32[2,1,32,256]{3,2,1,0:T(8,128)S(1)}, f32[2,1,32,256]{3,2,1,0:T(8,128)S(1)}, u32[]{:S(2)}, u32[]{:S(2)}) collective-permute-start(f32[2,1,32,256]{3,2,1,0:T(8,128)S(1)} %get-tuple-element.135), channel_id=1, source_target_pairs={{0,2},{1,3},{4,6},{5,7},{8,10},{9,11},{12,14},{13,15},{16,18},{17,... | collective-permute-start | bytes 196616 | tf_op jit(solution)/shard_map/ppermute | solution.py:23
  63.2 14.0 %all_gather.13 = f32[4,8,256]{2,0,1:T(4,128)S(1)} all-gather(f32[4,1,256]{2,0,1:T(4,128)S(1)} %slice.182), channel_id=1, replica_groups=mesh['groups'=2,'pipe'=4,'hour'=2,'seg'=2] {'pipe','seg'}, dimensions={1}, use_global_device_ids=true | all-gather | bytes 36864 | tf_op jit(solution)/shard_map/all_gather | solution.py:37
  77.5 0.7 gather_fusion.1
  78.7 2.2 collective-permute-start.6
  80.9 1.5 collective-permute-start.7
  82.7 1.4 collective-permute-done.7
  84.0 1.9 multiply_reduce_fusion.7
  86.1 1.3 collective-permute-start.9
  87.4 4.5 %collective-permute-start.8 = (f32[2,1,32,256]{3,2,1,0:T(8,128)S(1)}, f32[2,1,32,256]{3,2,1,0:T(8,128)S(1)}, u32[]{:S(2)}, u32[]{:S(2)}) collective-permute-start(f32[2,1,32,256]{3,2,1,0:T(8,128)S(1)} %get-tuple-element.131), channel_id=1, source_target_pairs={{0,2},{1,3},{4,6},{5,7},{8,10},{9,11},{12,14},{13,15},{16,18},{17,... | collective-permute-start | bytes 196616 | tf_op jit(solution)/shard_map/ppermute | solution.py:23
  91.9 4.5 %all-to-all-start.1 = ((f32[4,32,256]{2,0,1:T(4,128)}), f32[4,32,256]{2,0,1:T(4,128)S(1)}, u32[]{:S(2)}, u32[]{:S(2)}) async-start(f32[4,32,256]{2,0,1:T(4,128)} %multiply_subtract_fusion.3), calls=%async_computation.1 | async-start | bytes 262144 | tf_op jit(solution)/shard_map/all_to_all | solution.py:160
  98.4 14.6 %all_gather.14 = f32[4,8,256]{2,0,1:T(4,128)S(1)} all-gather(f32[4,1,256]{2,0,1:T(4,128)S(1)} %slice.191), channel_id=1, replica_groups=mesh['groups'=2,'pipe'=4,'hour'=2,'seg'=2] {'pipe','seg'}, dimensions={1}, use_global_device_ids=true | all-gather | bytes 36864 | tf_op jit(solution)/shard_map/all_gather | solution.py:37
  113.2 0.7 gather_fusion.2
  115.6 2.2 collective-permute-start.11
  117.8 0.8 copy.197
  118.6 1.3 collective-permute-start.10
  120.0 2.2 fusion.73
  122.2 2.1 fusion.1
  124.3 1.6 copy.174
  126.0 3.1 %reshape.118 = f32[4,1,8192]{2,1,0:T(1,128)} reshape(f32[1024,4,8]{2,1,0:T(4,128)S(1)} %bitcast.197) | data formatting | bytes 262144
  129.0 4.5 %all-to-all-start.2 = ((f32[4,1,8192]{2,1,0:T(1,128)}), f32[4,1,8192]{2,1,0:T(1,128)S(1)}, u32[]{:S(2)}, u32[]{:S(2)}) async-start(f32[4,1,8192]{2,1,0:T(1,128)} %reshape.118), calls=%async_computation.2 | async-start | bytes 262144 | tf_op jit(solution)/shard_map/all_to_all | solution.py:142
  133.6 1.0 fusion.31
  135.3 7.7 %all-reduce.1 = (f32[]{:T(128)}, f32[]{:T(128)}) all-reduce(f32[]{:T(128)S(6)} %add.161, f32[]{:T(128)S(6)} %add.163), channel_id=1, replica_groups=mesh['groups'=2,'pipe'=4,'hour'=2,'seg'=2] {'hour','seg'}, use_global_device_ids=true, to_apply=%region_5.7 | all-reduce | flops 2 | bytes 16 | tf_op jit(solution)/shard_map/psum | solution.py:173
  143.0 12.5 %all-reduce.3 = (f32[]{:T(128)}, f32[]{:T(128)}) all-reduce(f32[]{:T(128)} %get-tuple-element.99, f32[]{:T(128)} %get-tuple-element.100), channel_id=1, replica_groups=mesh['groups'=2,'pipe'=4,'hour'=2,'seg'=2] {'pipe'}, use_global_device_ids=true, to_apply=%region_6.8 | all-reduce | flops 2 | bytes 16 | tf_op jit(solution)/shard_map/psum | solution.py:172
  157.0 1.0 reduce.1
  158.0 2.5 %reshape.119 = f32[1024,4,8]{2,1,0:T(4,128)S(1)} reshape(f32[4,8192]{1,0:T(4,128)S(1)} %reduce.1) | data formatting | bytes 262144
  160.5 1.8 broadcast_multiply_fusion
  162.3 1.9 copy.175
  164.2 0.9 multiply_reduce_fusion
  165.2 0.7 multiply_subtract_fusion.1
  165.9 0.9 copy_dynamic-update-slice_fusion
  166.9 1.3 collective-permute-start.13
  168.2 4.5 %collective-permute-start.12 = (f32[2,1,32,256]{3,2,1,0:T(8,128)S(1)}, f32[2,1,32,256]{3,2,1,0:T(8,128)S(1)}, u32[]{:S(2)}, u32[]{:S(2)}) collective-permute-start(f32[2,1,32,256]{3,2,1,0:T(8,128)S(1)} %get-tuple-element.127), channel_id=1, source_target_pairs={{0,2},{1,3},{4,6},{5,7},{8,10},{9,11},{12,14},{13,15},{16,18},{17,... | collective-permute-start | bytes 196616 | tf_op jit(solution)/shard_map/ppermute | solution.py:23
  172.7 0.7 copy.186
  174.1 3.5 %all-to-all-start.3 = ((f32[4,32,256]{2,0,1:T(4,128)}), f32[4,32,256]{2,0,1:T(4,128)S(1)}, u32[]{:S(2)}, u32[]{:S(2)}) async-start(f32[4,32,256]{2,0,1:T(4,128)} %multiply_subtract_fusion.1), calls=%async_computation.3 | async-start | bytes 262144 | tf_op jit(solution)/shard_map/all_to_all | solution.py:160
  177.6 14.6 %all_gather.15 = f32[4,8,256]{2,0,1:T(4,128)S(1)} all-gather(f32[4,1,256]{2,0,1:T(4,128)S(1)} %slice.198), channel_id=1, replica_groups=mesh['groups'=2,'pipe'=4,'hour'=2,'seg'=2] {'pipe','seg'}, dimensions={1}, use_global_device_ids=true | all-gather | bytes 36864 | tf_op jit(solution)/shard_map/all_gather | solution.py:37
  192.5 0.7 gather_fusion.3
  194.8 1.3 collective-permute-start.15
  196.3 3.0 %collective-permute-start.14 = (f32[2,6,1,256]{1,3,2,0:T(8,128)S(1)}, f32[2,6,1,256]{1,3,2,0:T(8,128)S(1)}, u32[]{:S(2)}, u32[]{:S(2)}) collective-permute-start(f32[2,6,1,256]{1,3,2,0:T(8,128)S(1)} %copy.201), channel_id=1, source_target_pairs={{0,1},{2,3},{4,5},{6,7},{8,9},{10,11},{12,13},{14,15},{16,17},{18,... | collective-permute-start | bytes 36872 | tf_op jit(solution)/shard_map/ppermute | solution.py:23
  199.4 1.1 collective-permute-done.14
  200.7 1.8 multiply_reduce_fusion.2
  204.6 2.4 %multiply_reduce_fusion.8 = (f32[]{:T(128)}, f32[4,8,128]{2,1,0:T(8,128)}) fusion(f32[4,8,128]{2,1,0:T(8,128)S(1)} %get-tuple-element.142, f32[4,8,1024]{2,1,0:T(8,128)S(1)} %bitcast.215, s32[4,1024]{1,0:T(4,128)S(1)} %copy-done.15, f32[4,1,8,128]{3,2,1,0:T(8,128)S(1)} %copy-done.16, f32[]{:T(128)S(6)} %mul.158), kind=kOutput, calls=%fused_computation.134 | convolution fusion | flops 50884608 | bytes 196616 | tf_op jit(solution)/shard_map/while/body/eval_jaxpr/hsp,hpc->hsc/dot_general | solution.py:56
  208.3 6.5 %all-reduce = (f32[]{:T(128)}, f32[]{:T(128)}) all-reduce(f32[]{:T(128)S(6)} %add.175, f32[]{:T(128)S(6)} %add.177), channel_id=1, replica_groups=mesh['groups'=2,'pipe'=4,'hour'=2,'seg'=2] {'hour','seg'}, use_global_device_ids=true, to_apply=%region_14.16 | all-reduce | flops 2 | bytes 16 | tf_op jit(solution)/shard_map/psum | solution.py:173
  214.8 12.1 %all-reduce.2 = (f32[]{:T(128)}, f32[]{:T(128)}) all-reduce(f32[]{:T(128)} %get-tuple-element.97, f32[]{:T(128)} %get-tuple-element.98), channel_id=1, replica_groups=mesh['groups'=2,'pipe'=4,'hour'=2,'seg'=2] {'pipe'}, use_global_device_ids=true, to_apply=%region_15.17 | all-reduce | flops 2 | bytes 16 | tf_op jit(solution)/shard_map/psum | solution.py:172
  (121 shorter events, 7.9 us)
Async XLA Ops:
  2.8 10.3 %copy-start = (f32[4,32,256]{2,1,0:T(8,128)S(1)}, f32[4,32,256]{2,1,0:T(8,128)}, u32[]{:S(2)}) copy-start(f32[4,32,256]{2,1,0:T(8,128)} %param.16) | copy-start | bytes 393220
  2.8 10.3 %copy-start.1 = (f32[4,32,256]{2,1,0:T(8,128)S(1)}, f32[4,32,256]{2,1,0:T(8,128)}, u32[]{:S(2)}) copy-start(f32[4,32,256]{2,1,0:T(8,128)} %param.17) | copy-start | bytes 393220
  3.7 30.2 %copy-start.12 = (s32[1024]{0:T(1024)S(1)}, s32[1024]{0:T(1024)}, u32[]{:S(2)}) copy-start(s32[1024]{0:T(1024)} %param.24) | copy-start | bytes 12292
  3.7 35.3 %copy-start.11 = (s32[32,256]{1,0:T(8,128)S(1)}, s32[32,256]{1,0:T(8,128)}, u32[]{:S(2)}) copy-start(s32[32,256]{1,0:T(8,128)} %param.23) | copy-start | bytes 98308
  3.7 35.3 %copy-start.13 = (f32[16]{0:T(128)S(1)}, f32[16]{0:T(128)}, u32[]{:S(2)}) copy-start(f32[16]{0:T(128)} %param.22) | copy-start | bytes 196
  6.8 39.5 %all-to-all-start = ((f32[4,1,8192]{2,1,0:T(1,128)}), f32[4,1,8192]{2,1,0:T(1,128)S(1)}, u32[]{:S(2)}, u32[]{:S(2)}) async-start(f32[4,1,8192]{2,1,0:T(1,128)} %reshape.116), calls=%async_computation | async-start | bytes 262144 | tf_op jit(solution)/shard_map/all_to_all | solution.py:142
  13.2 26.8 %collective-permute-start.1 = (f32[2,1,32,256]{3,2,1,0:T(8,128)S(1)}, f32[2,1,32,256]{3,2,1,0:T(8,128)S(1)}, u32[]{:S(2)}, u32[]{:S(2)}) collective-permute-start(f32[2,1,32,256]{3,2,1,0:T(8,128)S(1)} %get-tuple-element.140), channel_id=1, source_target_pairs={{2,0},{3,1},{6,4},{7,5},{10,8},{11,9},{14,12},{15,13},{18,16},{19,... | collective-permute-start | bytes 196616 | tf_op jit(solution)/shard_map/ppermute | solution.py:25
  14.5 25.5 %collective-permute-start = (f32[2,1,32,256]{3,2,1,0:T(8,128)S(1)}, f32[2,1,32,256]{3,2,1,0:T(8,128)S(1)}, u32[]{:S(2)}, u32[]{:S(2)}) collective-permute-start(f32[2,1,32,256]{3,2,1,0:T(8,128)S(1)} %get-tuple-element.139), channel_id=1, source_target_pairs={{0,2},{1,3},{4,6},{5,7},{8,10},{9,11},{12,14},{13,15},{16,18},{17,... | collective-permute-start | bytes 196616 | tf_op jit(solution)/shard_map/ppermute | solution.py:23
  40.3 13.8 %collective-permute-start.3 = (f32[2,6,1,256]{3,1,2,0:T(8,128)S(1)}, f32[2,6,1,256]{3,1,2,0:T(8,128)S(1)}, u32[]{:S(2)}, u32[]{:S(2)}) collective-permute-start(f32[2,6,1,256]{3,1,2,0:T(8,128)S(1)} %slice.177), channel_id=1, source_target_pairs={{0,1},{2,3},{4,5},{6,7},{8,9},{10,11},{12,13},{14,15},{16,17},{18,... | collective-permute-start | bytes 36872 | tf_op jit(solution)/shard_map/ppermute | solution.py:23
  42.7 3.4 %collective-permute-start.2 = (f32[2,6,1,256]{1,3,2,0:T(8,128)S(1)}, f32[2,6,1,256]{1,3,2,0:T(8,128)S(1)}, u32[]{:S(2)}, u32[]{:S(2)}) collective-permute-start(f32[2,6,1,256]{1,3,2,0:T(8,128)S(1)} %copy.191), channel_id=1, source_target_pairs={{1,0},{3,2},{5,4},{7,6},{9,8},{11,10},{13,12},{15,14},{17,16},{19,... | collective-permute-start | bytes 36872 | tf_op jit(solution)/shard_map/ppermute | solution.py:25
  52.1 1.9 copy-start.2
  52.1 2.0 copy-start.3
  52.1 2.0 copy-start.4
  52.1 2.0 copy-start.8
  52.1 2.0 copy-start.9
  57.2 26.8 %copy-start.6 = (f32[4,32,256]{2,1,0:T(8,128)S(1)}, f32[4,32,256]{2,1,0:T(8,128)}, u32[]{:S(2)}) copy-start(f32[4,32,256]{2,1,0:T(8,128)} %param.20) | copy-start | bytes 393220
  57.2 21.0 %collective-permute-start.5 = (f32[2,1,32,256]{3,2,1,0:T(8,128)S(1)}, f32[2,1,32,256]{3,2,1,0:T(8,128)S(1)}, u32[]{:S(2)}, u32[]{:S(2)}) collective-permute-start(f32[2,1,32,256]{3,2,1,0:T(8,128)S(1)} %get-tuple-element.136), channel_id=1, source_target_pairs={{2,0},{3,1},{6,4},{7,5},{10,8},{11,9},{14,12},{15,13},{18,16},{19,... | collective-permute-start | bytes 196616 | tf_op jit(solution)/shard_map/ppermute | solution.py:25
  58.6 19.6 %collective-permute-start.4 = (f32[2,1,32,256]{3,2,1,0:T(8,128)S(1)}, f32[2,1,32,256]{3,2,1,0:T(8,128)S(1)}, u32[]{:S(2)}, u32[]{:S(2)}) collective-permute-start(f32[2,1,32,256]{3,2,1,0:T(8,128)S(1)} %get-tuple-element.135), channel_id=1, source_target_pairs={{0,2},{1,3},{4,6},{5,7},{8,10},{9,11},{12,14},{13,15},{16,18},{17,... | collective-permute-start | bytes 196616 | tf_op jit(solution)/shard_map/ppermute | solution.py:23
  78.7 3.7 %collective-permute-start.6 = (f32[2,6,1,256]{1,3,2,0:T(8,128)S(1)}, f32[2,6,1,256]{1,3,2,0:T(8,128)S(1)}, u32[]{:S(2)}, u32[]{:S(2)}) collective-permute-start(f32[2,6,1,256]{1,3,2,0:T(8,128)S(1)} %copy.195), channel_id=1, source_target_pairs={{0,1},{2,3},{4,5},{6,7},{8,9},{10,11},{12,13},{14,15},{16,17},{18,... | collective-permute-start | bytes 36872 | tf_op jit(solution)/shard_map/ppermute | solution.py:23
  80.9 3.1 %collective-permute-start.7 = (f32[2,6,1,256]{3,1,2,0:T(8,128)S(1)}, f32[2,6,1,256]{3,1,2,0:T(8,128)S(1)}, u32[]{:S(2)}, u32[]{:S(2)}) collective-permute-start(f32[2,6,1,256]{3,1,2,0:T(8,128)S(1)} %slice.185), channel_id=1, source_target_pairs={{1,0},{3,2},{5,4},{7,6},{9,8},{11,10},{13,12},{15,14},{17,16},{19,... | collective-permute-start | bytes 36872 | tf_op jit(solution)/shard_map/ppermute | solution.py:25
  86.0 33.9 %copy-start.14 = (f32[4,1,8,128]{3,2,1,0:T(8,128)S(1)}, f32[4,1,8,128]{3,2,1,0:T(8,128)}, u32[]{:S(2)}) copy-start(f32[4,1,8,128]{3,2,1,0:T(8,128)} %param.18) | copy-start | bytes 49156
  86.0 33.9 %copy-start.15 = (s32[4,1024]{1,0:T(4,128)S(1)}, s32[4,1024]{1,0:T(4,128)}, u32[]{:S(2)}) copy-start(s32[4,1024]{1,0:T(4,128)} %param.25) | copy-start | bytes 49156
  86.1 33.9 %copy-start.16 = (f32[4,1,8,128]{3,2,1,0:T(8,128)S(1)}, f32[4,1,8,128]{3,2,1,0:T(8,128)}, u32[]{:S(2)}) copy-start(f32[4,1,8,128]{3,2,1,0:T(8,128)} %param.21) | copy-start | bytes 49156
  86.1 29.1 %collective-permute-start.9 = (f32[2,1,32,256]{3,2,1,0:T(8,128)S(1)}, f32[2,1,32,256]{3,2,1,0:T(8,128)S(1)}, u32[]{:S(2)}, u32[]{:S(2)}) collective-permute-start(f32[2,1,32,256]{3,2,1,0:T(8,128)S(1)} %get-tuple-element.132), channel_id=1, source_target_pairs={{2,0},{3,1},{6,4},{7,5},{10,8},{11,9},{14,12},{15,13},{18,16},{19,... | collective-permute-start | bytes 196616 | tf_op jit(solution)/shard_map/ppermute | solution.py:25
  87.4 27.9 %collective-permute-start.8 = (f32[2,1,32,256]{3,2,1,0:T(8,128)S(1)}, f32[2,1,32,256]{3,2,1,0:T(8,128)S(1)}, u32[]{:S(2)}, u32[]{:S(2)}) collective-permute-start(f32[2,1,32,256]{3,2,1,0:T(8,128)S(1)} %get-tuple-element.131), channel_id=1, source_target_pairs={{0,2},{1,3},{4,6},{5,7},{8,10},{9,11},{12,14},{13,15},{16,18},{17,... | collective-permute-start | bytes 196616 | tf_op jit(solution)/shard_map/ppermute | solution.py:23
  91.9 28.0 %all-to-all-start.1 = ((f32[4,32,256]{2,0,1:T(4,128)}), f32[4,32,256]{2,0,1:T(4,128)S(1)}, u32[]{:S(2)}, u32[]{:S(2)}) async-start(f32[4,32,256]{2,0,1:T(4,128)} %multiply_subtract_fusion.3), calls=%async_computation.1 | async-start | bytes 262144 | tf_op jit(solution)/shard_map/all_to_all | solution.py:160
  115.6 48.6 %collective-permute-start.11 = (f32[2,6,1,256]{3,1,2,0:T(8,128)S(1)}, f32[2,6,1,256]{3,1,2,0:T(8,128)S(1)}, u32[]{:S(2)}, u32[]{:S(2)}) collective-permute-start(f32[2,6,1,256]{3,1,2,0:T(8,128)S(1)} %slice.193), channel_id=1, source_target_pairs={{0,1},{2,3},{4,5},{6,7},{8,9},{10,11},{12,13},{14,15},{16,17},{18,... | collective-permute-start | bytes 36872 | tf_op jit(solution)/shard_map/ppermute | solution.py:23
  118.6 14.9 %collective-permute-start.10 = (f32[2,6,1,256]{1,3,2,0:T(8,128)}, f32[2,6,1,256]{1,3,2,0:T(8,128)}, u32[]{:S(2)}, u32[]{:S(2)}) collective-permute-start(f32[2,6,1,256]{1,3,2,0:T(8,128)} %copy.197), channel_id=1, source_target_pairs={{1,0},{3,2},{5,4},{7,6},{9,8},{11,10},{13,12},{15,14},{17,16},{19,... | collective-permute-start | bytes 36872 | tf_op jit(solution)/shard_map/ppermute | solution.py:25
  129.0 27.9 %all-to-all-start.2 = ((f32[4,1,8192]{2,1,0:T(1,128)}), f32[4,1,8192]{2,1,0:T(1,128)S(1)}, u32[]{:S(2)}, u32[]{:S(2)}) async-start(f32[4,1,8192]{2,1,0:T(1,128)} %reshape.118), calls=%async_computation.2 | async-start | bytes 262144 | tf_op jit(solution)/shard_map/all_to_all | solution.py:142
  162.3 1.9 copy-start.5
  162.3 1.9 copy-start.10
  166.9 27.6 %collective-permute-start.13 = (f32[2,1,32,256]{3,2,1,0:T(8,128)S(1)}, f32[2,1,32,256]{3,2,1,0:T(8,128)S(1)}, u32[]{:S(2)}, u32[]{:S(2)}) collective-permute-start(f32[2,1,32,256]{3,2,1,0:T(8,128)S(1)} %get-tuple-element.128), channel_id=1, source_target_pairs={{2,0},{3,1},{6,4},{7,5},{10,8},{11,9},{14,12},{15,13},{18,16},{19,... | collective-permute-start | bytes 196616 | tf_op jit(solution)/shard_map/ppermute | solution.py:25
  168.2 26.3 %collective-permute-start.12 = (f32[2,1,32,256]{3,2,1,0:T(8,128)S(1)}, f32[2,1,32,256]{3,2,1,0:T(8,128)S(1)}, u32[]{:S(2)}, u32[]{:S(2)}) collective-permute-start(f32[2,1,32,256]{3,2,1,0:T(8,128)S(1)} %get-tuple-element.127), channel_id=1, source_target_pairs={{0,2},{1,3},{4,6},{5,7},{8,10},{9,11},{12,14},{13,15},{16,18},{17,... | collective-permute-start | bytes 196616 | tf_op jit(solution)/shard_map/ppermute | solution.py:23
  174.1 26.6 %copy-start.7 = (f32[4,32,256]{2,1,0:T(8,128)S(1)}, f32[4,32,256]{2,1,0:T(8,128)}, u32[]{:S(2)}) copy-start(f32[4,32,256]{2,1,0:T(8,128)} %param.20) | copy-start | bytes 393220
  174.1 30.4 %all-to-all-start.3 = ((f32[4,32,256]{2,0,1:T(4,128)}), f32[4,32,256]{2,0,1:T(4,128)S(1)}, u32[]{:S(2)}, u32[]{:S(2)}) async-start(f32[4,32,256]{2,0,1:T(4,128)} %multiply_subtract_fusion.1), calls=%async_computation.3 | async-start | bytes 262144 | tf_op jit(solution)/shard_map/all_to_all | solution.py:160
  194.8 5.8 %collective-permute-start.15 = (f32[2,6,1,256]{3,1,2,0:T(8,128)S(1)}, f32[2,6,1,256]{3,1,2,0:T(8,128)S(1)}, u32[]{:S(2)}, u32[]{:S(2)}) collective-permute-start(f32[2,6,1,256]{3,1,2,0:T(8,128)S(1)} %slice.201), channel_id=1, source_target_pairs={{1,0},{3,2},{5,4},{7,6},{9,8},{11,10},{13,12},{15,14},{17,16},{19,... | collective-permute-start | bytes 36872 | tf_op jit(solution)/shard_map/ppermute | solution.py:25
  196.3 4.2 %collective-permute-start.14 = (f32[2,6,1,256]{1,3,2,0:T(8,128)S(1)}, f32[2,6,1,256]{1,3,2,0:T(8,128)S(1)}, u32[]{:S(2)}, u32[]{:S(2)}) collective-permute-start(f32[2,6,1,256]{1,3,2,0:T(8,128)S(1)} %copy.201), channel_id=1, source_target_pairs={{0,1},{2,3},{4,5},{6,7},{8,9},{10,11},{12,13},{14,15},{16,17},{18,... | collective-permute-start | bytes 36872 | tf_op jit(solution)/shard_map/ppermute | solution.py:23
